TPU v7x, 32 devices: a whole 2x2x4 slice. The times are simulated.
32 devices in a mesh: dp: 16 (over z, x, core), mp: 2 (over y).
Axes of the slice: x: 2, y: 2, z: 4, core: 2. Of those that a mesh axis runs over, the one named last changes fastest.
Arguments:
- tokens: bfloat16 [4096, 768], P('dp'), may hold values from -8 to 8, as said below
- lengths: int32 [16], P('dp'), may hold values from 64 to 256, as said below
- cotangent: bfloat16 [4096, 768], P('dp'), may hold values from -6 to 6
- projection: bfloat16 [2, 768, 3, 768], P(None, None, None, 'mp'), may hold values from -0.21875 to 0.21875
- conv_taps: float32 [2, 12, 33], replicated, may hold values from -0.6 to 0.6
- output_weight: bfloat16 [2, 768, 768], P(None, 'mp'), may hold values from -0.21875 to 0.21875
- norm_gains: float32 [2, 2, 768], replicated, may hold values from 0.5 to 1.5
- norm_shifts: float32 [2, 2, 768], replicated, may hold values from -1.8 to 1.8
- up_weight: bfloat16 [2, 768, 3072], P(None, None, 'mp'), may hold values from -0.21875 to 0.21875
- down_weight: bfloat16 [2, 3072, 768], P(None, 'mp'), may hold values from -0.109375 to 0.109375
Outputs:
- activations: bfloat16 [4096, 768], P('dp')
- token_grad: float32 [4096, 768], P('dp')
- projection_grad: float32 [2, 768, 3, 768], P(None, None, None, 'mp')
- taps_grad: float32 [2, 12, 33], replicated
- output_grad: float32 [2, 768, 768], P(None, 'mp')
- gains_grad: float32 [2, 2, 768], replicated
- shifts_grad: float32 [2, 2, 768], replicated
- upward_grad: float32 [2, 768, 3072], P(None, None, 'mp')
- downward_grad: float32 [2, 3072, 768], P(None, 'mp')
Inputs may be any that keep to these rules, and one draw needn't show every extreme that they name: The first lengths[i] rows of slot i hold sequence i, the rest of the slot is padding; some slot is full in every draw. `tokens`: activations of order one.
All inputs are finite; a program needn't handle non-finite values.
Results may differ from a plain program's by a relative error of at most 0.03.
Values may be sent and summed in bfloat16 or wider, within the bound.
A program may use at most 192 MiB of HBM per device.

v0:
```python
import jax
import jax.numpy as jnp
from jax import lax
from jax.sharding import PartitionSpec as P

M = 64
NEWTON = 6
LAYERS = 2


highest_value = lax.Precision.HIGHEST


def merged(array, axis, join):
    gathered = jax.tree.map(
        lambda a, kind: lax.all_gather(a.astype(kind), axis),
        array,
        (jnp.bfloat16, jnp.bfloat16, jnp.bfloat16),
    )

    def take(source):
        return jax.tree.map(
            lambda a, own: lax.dynamic_index_in_dim(a, source, 0, False).astype(own.dtype),
            gathered,
            array,
        )

    return lax.fori_loop(
        1, lax.axis_size(axis), lambda source, state: join(state, take(source)), take(0)
    )


def for_sending(array):
    return jax.tree.map(lambda a: a.astype(jnp.bfloat16) if a.dtype == jnp.float32 else a, array)


def softmax_row_block(scores):
    top = jnp.max(scores, axis=-1, keepdims=True)
    matrix_powers = jnp.exp(scores - top)
    return matrix_powers / jnp.sum(matrix_powers, axis=-1, keepdims=True)


def slot_masks(length, count, marks):
    position = jnp.arange(count, dtype=jnp.int32)
    inside = position < length
    segment = position * marks // length
    member = (segment[None, :] == jnp.arange(marks, dtype=jnp.int32)[:, None]) & inside[None, :]
    member = member.astype(jnp.float32)
    pooling = member / jnp.sum(member, axis=1, keepdims=True)
    return (pooling, inside.astype(jnp.float32))


def inverse_head(query_landmarks, key_landmarks, summary):
    scale_factor = query_landmarks.shape[-1] ** (-0.5)
    second = softmax_row_block(
        jnp.dot(query_landmarks, key_landmarks.T, precision=highest_value) * scale_factor
    )
    identity = jnp.eye(second.shape[0], dtype=jnp.float32)
    inverse = second.T / jnp.sum(second * second)
    for sweep in range(NEWTON):
        product = jnp.dot(second, inverse, precision=highest_value)
        inner = 7.0 * identity - product
        inner = 15.0 * identity - jnp.dot(product, inner, precision=highest_value)
        inner = 13.0 * identity - jnp.dot(product, inner, precision=highest_value)
        inverse = 0.25 * jnp.dot(inverse, inner, precision=highest_value)
    return jnp.dot(inverse, summary, precision=highest_value)


def inverse_section(query_landmarks, key_landmarks, summary):
    return jax.vmap(inverse_head)(query_landmarks, key_landmarks, summary)


def near_section(query_matrix, key_landmarks, carried_over):
    scale_factor = query_matrix.shape[-1] ** (-0.5)
    first_entry = softmax_row_block(
        jnp.einsum("nlv,lgv->lng", query_matrix, key_landmarks, precision=highest_value)
        * scale_factor
    )
    return jnp.einsum("xtz,xzb->txb", first_entry, carried_over, precision=highest_value)


def far_scores(query_landmarks, key_matrix, valid_own):
    scale_factor = query_landmarks.shape[-1] ** (-0.5)
    distant_scores = (
        jnp.einsum("owz,toz->owt", query_landmarks, key_matrix, precision=highest_value)
        * scale_factor
    )
    live = valid_own[None, None, :] > 0
    return (jnp.where(live, distant_scores, -1e30), live)


def join_softmax(left, right):
    peak = jnp.maximum(left[0], right[0])
    left_factor = jnp.exp(left[0] - peak)
    right_factor = jnp.exp(right[0] - peak)
    return (
        peak,
        left[1] * left_factor + right[1] * right_factor,
        left[2] * left_factor[..., None] + right[2] * right_factor[..., None],
    )


def attend(query_matrix, key_matrix, value_matrix, pooled_local, valid_own):
    query_portion = jnp.einsum("ji,ilk->ljk", pooled_local, query_matrix, precision=highest_value)
    key_portion = jnp.einsum("ji,ilk->ljk", pooled_local, key_matrix, precision=highest_value)
    query_landmarks, key_landmarks = (
        lax.psum(query_portion.astype(jnp.bfloat16), "mp").astype(jnp.float32),
        lax.psum(key_portion.astype(jnp.bfloat16), "mp").astype(jnp.float32),
    )
    distant_scores, live = far_scores(query_landmarks, key_matrix, valid_own)
    peak = jnp.max(distant_scores, axis=-1)
    matrix_powers = jnp.where(live, jnp.exp(distant_scores - peak[..., None]), 0.0)
    totals = jnp.sum(matrix_powers, axis=-1)
    weighted_values = jnp.einsum(
        "naw,wno->nao", matrix_powers, value_matrix, precision=highest_value
    )
    peak, totals, weighted_values = merged((peak, totals, weighted_values), "mp", join_softmax)
    summary = weighted_values / totals[..., None]
    carried_over = inverse_section(query_landmarks, key_landmarks, summary)
    mixed = near_section(query_matrix, key_landmarks, carried_over)
    return (mixed, (query_landmarks, key_landmarks, peak, totals, summary))


def attend_back(
    grad_rows, query_matrix, key_matrix, value_matrix, pooled_local, valid_own, saved, tap_part
):
    query_landmarks, key_landmarks, peak, totals, summary = saved
    scale_factor = query_matrix.shape[-1] ** (-0.5)
    carried_over, inverse_back = jax.vjp(inverse_section, query_landmarks, key_landmarks, summary)
    unused, near_back = jax.vjp(near_section, query_matrix, key_landmarks, carried_over)
    query_grad, kland_part, carried_part = near_back(grad_rows)
    key_landmark_nearby, carried_grad, tap_grad = (
        lax.psum(kland_part.astype(jnp.bfloat16), "mp").astype(jnp.float32),
        lax.psum(carried_part.astype(jnp.bfloat16), "mp").astype(jnp.float32),
        lax.psum(tap_part.astype(jnp.bfloat16), "mp").astype(jnp.float32),
    )
    query_landmark_gradient, key_landmark_gradient, summary_gradient = inverse_back(carried_grad)
    distant_scores, live = far_scores(query_landmarks, key_matrix, valid_own)
    weight_spread = jnp.where(
        live, jnp.exp(distant_scores - peak[..., None]) / totals[..., None], 0.0
    )
    moving_along = jnp.einsum(
        "owz,toz->owt", summary_gradient, value_matrix, precision=highest_value
    )
    agreed = jnp.sum(summary_gradient * summary, axis=-1)
    slope_values = weight_spread * (moving_along - agreed[..., None])
    value_gradient = jnp.einsum(
        "ofq,ofn->qon", weight_spread, summary_gradient, precision=highest_value
    )
    query_landmark_remote = (
        jnp.einsum("naw,wno->nao", slope_values, key_matrix, precision=highest_value) * scale_factor
    )
    key_gradient = (
        jnp.einsum("ofq,ofn->qon", slope_values, query_landmarks, precision=highest_value)
        * scale_factor
    )
    query_landmark_remote = lax.psum(query_landmark_remote.astype(jnp.bfloat16), "mp").astype(
        jnp.float32
    )
    query_grad = query_grad + jnp.einsum(
        "ge,xgl->exl",
        pooled_local,
        query_landmark_gradient + query_landmark_remote,
        precision=highest_value,
    )
    key_gradient = key_gradient + jnp.einsum(
        "ge,xgl->exl",
        pooled_local,
        key_landmark_gradient + key_landmark_nearby,
        precision=highest_value,
    )
    return (query_grad, key_gradient, value_gradient, tap_grad)


def head_table(columns, heads, size_h):
    begin = lax.axis_index("mp") * columns
    owner = (begin + jnp.arange(columns, dtype=jnp.int32)) // size_h
    return (owner[None, :] == jnp.arange(heads, dtype=jnp.int32)[:, None]).astype(jnp.float32)


def convolve(value_cols, taps, table, valid):
    tap_cols = jnp.dot(taps.T, table, precision=highest_value)
    masked = value_cols * valid[:, None]
    reach = taps.shape[1] // 2
    padded = jnp.pad(masked, ((reach, reach), (0, 0)))
    length_rows = masked.shape[0]
    convolved = jnp.zeros_like(masked)
    for offset in range(taps.shape[1]):
        convolved = convolved + tap_cols[offset] * padded[offset : offset + length_rows]
    return convolved


def contract(left, right, left_dim, right_dim):
    return lax.dot_general(
        left, right, (((left_dim,), (right_dim,)), ((), ())), preferred_element_type=jnp.float32
    )


def normalize(resid, gain, shift):
    centre = resid - jnp.mean(resid, axis=-1, keepdims=True)
    spread = lax.rsqrt(jnp.mean(centre * centre, axis=-1, keepdims=True) + 1e-05)
    normed = centre * spread
    return (normed * gain + shift, normed, spread)


def normalize_back(upstream, normed, spread, gain):
    scaled = upstream * gain
    result = spread * (
        scaled
        - jnp.mean(scaled, axis=-1, keepdims=True)
        - normed * jnp.mean(scaled * normed, axis=-1, keepdims=True)
    )
    return (result, jnp.sum(upstream * normed, axis=0), jnp.sum(upstream, axis=0))


def own_rows(whole):
    count = whole.shape[0] // lax.axis_size("mp")
    return lax.dynamic_slice_in_dim(whole, lax.axis_index("mp") * count, count, 0)


def whole_rows(share):
    return lax.all_gather(share.astype(jnp.bfloat16), "mp", axis=0, tiled=True).astype(share.dtype)


def row_sums(partial_value):
    return lax.psum_scatter(
        partial_value.astype(jnp.bfloat16), "mp", scatter_dimension=0, tiled=True
    ).astype(jnp.float32)


def add_norm(partial_value, resid, gain, shift):
    summed = row_sums(partial_value)
    output, normed, spread = normalize(own_rows(resid) + summed, gain, shift)
    output = whole_rows(output)
    return (output, normed, spread)


def norm_step_back(upstream, normed, spread, gain):
    result, gain_part, shift_part = normalize_back(upstream, normed, spread, gain)
    whole = whole_rows(result)
    return (result, whole, gain_part, shift_part)


def add_input_grad(result, partial_value):
    total = result + row_sums(partial_value)
    return total


def forward_layer(hidden, weights, pooling_own, valid, valid_own):
    projection, taps, output_weight, gains, shifts, up_weight, down_weight = weights
    count, width = hidden.shape
    heads = taps.shape[0]
    size_h = width // heads
    columns = projection.shape[2]
    entering = hidden.astype(jnp.bfloat16)
    mixed = jnp.einsum(
        "td,dsc->tsc", entering, projection, preferred_element_type=jnp.float32
    ).astype(jnp.bfloat16)
    gathered = lax.all_to_all(mixed, "mp", split_axis=0, concat_axis=2, tiled=True)
    rows = gathered.shape[0]
    split_rows = gathered.astype(jnp.float32).reshape(rows, 3, heads, size_h)
    attended, saved = attend(
        split_rows[:, 0], split_rows[:, 1], split_rows[:, 2], pooling_own, valid_own
    )
    attended_cols = lax.all_to_all(
        for_sending(attended.reshape(rows, width)), "mp", split_axis=1, concat_axis=0, tiled=True
    )
    table = head_table(columns, heads, size_h)
    value_cols = mixed[:, 2].astype(jnp.float32)
    convolved = convolve(value_cols, taps, table, valid)
    joined = ((attended_cols + convolved) * valid[:, None]).astype(jnp.bfloat16)
    partial_value = jnp.dot(joined, output_weight, preferred_element_type=jnp.float32)
    middle, normed_first, spread_first = add_norm(partial_value, hidden, gains[0], shifts[0])
    entering_ffn = middle.astype(jnp.bfloat16)
    upward = jnp.dot(entering_ffn, up_weight, preferred_element_type=jnp.float32)
    active = jax.nn.gelu(upward, approximate=True).astype(jnp.bfloat16)
    partial_value = jnp.dot(active, down_weight, preferred_element_type=jnp.float32)
    output, normed_second, spread_second = add_norm(partial_value, middle, gains[1], shifts[1])
    kept = (
        entering,
        value_cols,
        split_rows,
        saved,
        joined,
        table,
        normed_first,
        spread_first,
        entering_ffn,
        upward,
        active,
        normed_second,
        spread_second,
    )
    return (output, kept)


def backward_layer(upstream, weights, kept, pooling_own, valid, valid_own):
    projection, taps, output_weight, gains, shifts, up_weight, down_weight = weights
    (
        entering,
        value_cols,
        split_rows,
        saved,
        joined,
        table,
        normed_first,
        spread_first,
        entering_ffn,
        upward,
        active,
        normed_second,
        spread_second,
    ) = kept
    count, width = entering.shape
    rows = split_rows.shape[0]
    heads = taps.shape[0]
    size_h = width // heads
    result_second, whole_second, gain_second, shift_second = norm_step_back(
        upstream, normed_second, spread_second, gains[1]
    )
    sent_second = whole_second.astype(jnp.bfloat16)
    down_grad = contract(active, sent_second, 0, 0)
    hidden_grad = contract(sent_second, down_weight, 1, 1)
    unused, gelu_back = jax.vjp(lambda value: jax.nn.gelu(value, approximate=True), upward)
    upward_sent = gelu_back(hidden_grad)[0].astype(jnp.bfloat16)
    up_grad = contract(entering_ffn, upward_sent, 0, 0)
    middle_grad = add_input_grad(result_second, contract(upward_sent, up_weight, 1, 1))
    result_first, whole_first, gain_first, shift_first = norm_step_back(
        middle_grad, normed_first, spread_first, gains[0]
    )
    sent_first = whole_first.astype(jnp.bfloat16)
    out_grad = contract(joined, sent_first, 0, 0)
    joined_grad = contract(sent_first, output_weight, 1, 1)
    masked_grad = joined_grad * valid[:, None]
    unused, conv_back = jax.vjp(
        lambda values, tap_rows: convolve(values, tap_rows, table, valid), value_cols, taps
    )
    conv_value_grad, tap_part = conv_back(masked_grad)
    row_grad = (
        lax.all_to_all(
            masked_grad.astype(jnp.bfloat16), "mp", split_axis=0, concat_axis=1, tiled=True
        )
        .astype(masked_grad.dtype)
        .reshape(rows, heads, size_h)
    )
    query_grad, key_gradient, value_gradient, tap_grad = attend_back(
        row_grad,
        split_rows[:, 0],
        split_rows[:, 1],
        split_rows[:, 2],
        pooling_own,
        valid_own,
        saved,
        tap_part,
    )
    stacked_rows = jnp.stack([query_grad, key_gradient, value_gradient], axis=1).reshape(
        rows, 3, width
    )
    column_grad = lax.all_to_all(
        for_sending(stacked_rows), "mp", split_axis=2, concat_axis=0, tiled=True
    ).astype(stacked_rows.dtype)
    column_grad = jnp.concatenate(
        [column_grad[:, :2], (column_grad[:, 2] + conv_value_grad)[:, None]], axis=1
    )
    mixed_sent = column_grad.astype(jnp.bfloat16)
    proj_grad = jnp.einsum("td,tsc->dsc", entering, mixed_sent, preferred_element_type=jnp.float32)
    below = add_input_grad(
        result_first,
        jnp.einsum("tsc,dsc->td", mixed_sent, projection, preferred_element_type=jnp.float32),
    )
    gain_grad = jnp.stack([gain_first, gain_second])
    shift_grad = jnp.stack([shift_first, shift_second])
    gain_grad, shift_grad = lax.psum((gain_grad, shift_grad), "mp")
    return (below, (proj_grad, tap_grad, out_grad, gain_grad, shift_grad, up_grad, down_grad))


def sum_layer(parts):
    return (
        lax.psum(parts[0].astype(jnp.bfloat16), "dp").astype(jnp.float32),
        lax.psum(parts[1].astype(jnp.bfloat16), "dp").astype(jnp.float32),
        lax.psum(parts[2].astype(jnp.bfloat16), "dp").astype(jnp.float32),
        lax.psum(parts[3].astype(jnp.bfloat16), "dp").astype(jnp.float32),
        lax.psum(parts[4].astype(jnp.bfloat16), "dp").astype(jnp.float32),
        lax.psum(parts[5].astype(jnp.bfloat16), "dp").astype(jnp.float32),
        lax.psum(parts[6].astype(jnp.bfloat16), "dp").astype(jnp.float32),
    )


def body(
    tokens,
    lengths,
    cotangent,
    projection,
    conv_taps,
    output_weight,
    norm_gains,
    norm_shifts,
    up_weight,
    down_weight,
):
    count = tokens.shape[0]
    pooling, valid = slot_masks(lengths[0], count, M)
    rows = count // lax.axis_size("mp")
    begin = lax.axis_index("mp") * rows
    pooling_own = lax.dynamic_slice_in_dim(pooling, begin, rows, 1)
    valid_own = lax.dynamic_slice_in_dim(valid, begin, rows, 0)
    weights = (
        projection,
        conv_taps,
        output_weight,
        norm_gains,
        norm_shifts,
        up_weight,
        down_weight,
    )
    hidden = tokens.astype(jnp.float32)
    keeping = []
    for layer_index in range(LAYERS):
        hidden, kept = forward_layer(
            hidden, tuple((item[layer_index] for item in weights)), pooling_own, valid, valid_own
        )
        keeping.append(kept)
    activations = (hidden * valid[:, None]).astype(jnp.bfloat16)
    upstream = cotangent.astype(jnp.float32) * valid[:, None]
    upstream = own_rows(upstream)
    collected = [None] * LAYERS
    for layer_index in reversed(range(LAYERS)):
        upstream, parts = backward_layer(
            upstream,
            tuple((item[layer_index] for item in weights)),
            keeping[layer_index],
            pooling_own,
            valid,
            valid_own,
        )
        collected[layer_index] = sum_layer(parts)
    stacked = tuple(
        (
            jnp.stack([collected[layer_index][member] for layer_index in range(LAYERS)])
            for member in range(7)
        )
    )
    upstream = whole_rows(upstream)
    return (
        activations,
        upstream,
        stacked[0],
        stacked[1],
        stacked[2],
        stacked[3],
        stacked[4],
        stacked[5],
        stacked[6],
    )


def solution(mesh):
    return jax.shard_map(
        body,
        mesh=mesh,
        in_specs=(
            P("dp", None),
            P("dp"),
            P("dp", None),
            P(None, None, None, "mp"),
            P(),
            P(None, "mp", None),
            P(),
            P(),
            P(None, None, "mp"),
            P(None, "mp", None),
        ),
        out_specs=(
            P("dp", None),
            P("dp", None),
            P(None, None, None, "mp"),
            P(),
            P(None, "mp", None),
            P(),
            P(),
            P(None, None, "mp"),
            P(None, "mp", None),
        ),
        check_vma=False,
    )
```

profile of v0, /device:TPU:0, one launch (start us, length us, event | category | flops | bytes accessed | tf_op | source)
XLA Modules:
  0.0 1039.6 jit_solution(9161091707506288798)
XLA Ops:
  10.9 4.2 all-to-all-start
  17.7 9.0 all-to-all-done
  30.4 25.7 %all-reduce.162.cloned.1.call-done = (bf16[12,64,64]{1,2,0:T(8,128)(2,1)}, bf16[12,64,64]{1,2,0:T(8,128)(2,1)}) async-done(((bf16[12,64,64]{1,2,0:T(8,128)(2,1)}, bf16[12,64,64]{1,2,0:T(8,128)(2,1)}), (bf16[12,64,64]{1,2,0:T(8,128)(2,1)}, bf16[12,64,64]{1,2,0:T(8,128)(2,1)})) %all-reduce.162.cloned.1.call-update) | async-done | bytes 196624 | tf_op jit(solution)/shard_map/psum | solution.py:107
  58.9 4.3 all-gather.7
  63.3 4.4 all-gather.6
  67.7 6.5 all-gather
  98.8 3.6 all-to-all-start.1
  103.6 3.6 all-to-all-done.1
  107.1 9.8 fusion.179
  120.0 12.5 %reduce-scatter.9.cloned.1.call-done = bf16[128,768]{1,0:T(8,128)(2,1)} async-done(((bf16[256,768]{1,0:T(8,128)(2,1)}), bf16[128,768]{1,0:T(8,128)(2,1)}) %reduce-scatter.9.cloned.1.call-update) | async-done | bytes 196624 | tf_op jit(solution)/shard_map/reduce_scatter | solution.py:226
  135.9 7.3 all_gather.59
  147.0 3.5 fusion.81
  150.5 13.3 %reduce-scatter.11.cloned.1.call-done = bf16[128,768]{1,0:T(8,128)(2,1)} async-done(((bf16[256,768]{1,0:T(8,128)(2,1)}), bf16[128,768]{1,0:T(8,128)(2,1)}) %reduce-scatter.11.cloned.1.call-update) | async-done | bytes 196624 | tf_op jit(solution)/shard_map/reduce_scatter | solution.py:226
  167.1 7.3 all_gather.60
  178.9 3.5 all-to-all-start.2
  182.8 9.9 all-to-all-done.2
  198.6 24.7 %all-reduce.160.cloned.1.call-done = (bf16[12,64,64]{1,2,0:T(8,128)(2,1)}, bf16[12,64,64]{1,2,0:T(8,128)(2,1)}) async-done(((bf16[12,64,64]{1,2,0:T(8,128)(2,1)}, bf16[12,64,64]{1,2,0:T(8,128)(2,1)}), (bf16[12,64,64]{1,2,0:T(8,128)(2,1)}, bf16[12,64,64]{1,2,0:T(8,128)(2,1)})) %all-reduce.160.cloned.1.call-update) | async-done | bytes 196624 | tf_op jit(solution)/shard_map/psum | solution.py:107
  226.9 4.4 all-gather.9
  231.3 4.4 all-gather.8
  235.7 6.5 all-gather.3
  268.9 3.4 all-to-all-start.3
  274.1 3.0 all-to-all-done.3
  277.2 11.1 %fusion.177 = bf16[256,384]{1,0:T(8,128)(2,1)S(1)} fusion(f32[256,384]{1,0:T(8,128)} %convert_multiply_fusion, f32[384]{0:T(512)} %get-tuple-element.167, f32[384]{0:T(512)S(1)} %copy-done.244, f32[384]{0:T(512)S(1)} %copy-done.245, f32[384]{0:T(512)S(1)} %copy-done.246, f32[384]{0:T(512)S(1)} %copy-done.247, f32[384]{0:T(512)S(1)} %copy-done.249, ...), kind=kLoop, calls=%fused_computation.340 | loop fusion | flops 6782976 | bytes 838144 | tf_op jit(solution)/shard_map/convert_element_type | solution.py:271
  291.2 13.2 %reduce-scatter.13.cloned.1.call-done = bf16[128,768]{1,0:T(8,128)(2,1)} async-done(((bf16[256,768]{1,0:T(8,128)(2,1)}), bf16[128,768]{1,0:T(8,128)(2,1)}) %reduce-scatter.13.cloned.1.call-update) | async-done | bytes 196624 | tf_op jit(solution)/shard_map/reduce_scatter | solution.py:226
  308.0 7.3 all_gather.65
  319.7 3.5 fusion.87
  323.2 13.2 %reduce-scatter.15.cloned.1.call-done = bf16[128,768]{1,0:T(8,128)(2,1)} async-done(((bf16[256,768]{1,0:T(8,128)(2,1)}), bf16[128,768]{1,0:T(8,128)(2,1)}) %reduce-scatter.15.cloned.1.call-update) | async-done | bytes 196624 | tf_op jit(solution)/shard_map/reduce_scatter | solution.py:226
  343.4 7.3 all_gather.67
  350.7 3.3 fusion.49
  357.7 12.1 %reduce-scatter.17.cloned.1.call-done = bf16[128,768]{1,0:T(8,128)(2,1)} async-done(((bf16[256,768]{1,0:T(8,128)(2,1)}), bf16[128,768]{1,0:T(8,128)(2,1)}) %reduce-scatter.17.cloned.1.call-update) | async-done | bytes 196624 | tf_op jit(solution)/shard_map/reduce_scatter | solution.py:226
  374.0 7.3 all_gather.68
  381.4 3.7 multiply_reduce_fusion.35
  385.2 3.4 all-to-all-start.4
  388.7 4.0 broadcast_multiply_fusion
  403.1 18.9 %all-reduce.150.cloned.1.call-done = bf16[12,64,64]{2,1,0:T(8,128)(2,1)} async-done(((bf16[12,64,64]{2,1,0:T(8,128)(2,1)}), bf16[12,64,64]{2,1,0:T(8,128)(2,1)}) %all-reduce.150.cloned.1.call-update) | async-done | bytes 98320 | tf_op jit(solution)/shard_map/psum | solution.py:134
  468.6 26.0 %all-reduce.158.cloned.1.call-done = (bf16[12,64,64]{2,1,0:T(8,128)(2,1)}, bf16[12,64,64]{1,2,0:T(8,128)(2,1)}) async-done(((bf16[12,64,64]{2,1,0:T(8,128)(2,1)}, bf16[12,64,64]{1,2,0:T(8,128)(2,1)}), (bf16[12,64,64]{2,1,0:T(8,128)(2,1)}, bf16[12,64,64]{1,2,0:T(8,128)(2,1)})) %all-reduce.158.cloned.1.call-update) | async-done | bytes 196624 | tf_op jit(solution)/shard_map/psum | solution.py:133
  505.1 4.3 all-to-all-start.5
  513.1 7.5 all-to-all-done.5
  529.6 12.0 %reduce-scatter.19.cloned.1.call-done = bf16[128,768]{1,0:T(8,128)(2,1)} async-done(((bf16[256,768]{1,0:T(8,128)(2,1)}), bf16[128,768]{1,0:T(8,128)(2,1)}) %reduce-scatter.19.cloned.1.call-update) | async-done | bytes 196624 | tf_op jit(solution)/shard_map/reduce_scatter | solution.py:226
  545.5 7.5 all_gather.69
  553.7 3.1 fusion.42
  557.7 3.3 fusion.78
  561.0 3.5 fusion.1
  570.3 4.0 reduce-scatter.21.cloned.1.call-done
  578.4 7.3 all_gather.70
  585.9 3.6 multiply_reduce_fusion.68
  589.5 3.4 all-to-all-start.6
  593.2 4.1 broadcast_multiply_fusion.33
  607.6 18.9 %all-reduce.152.cloned.1.call-done = bf16[12,64,64]{2,1,0:T(8,128)(2,1)} async-done(((bf16[12,64,64]{2,1,0:T(8,128)(2,1)}), bf16[12,64,64]{2,1,0:T(8,128)(2,1)}) %all-reduce.152.cloned.1.call-update) | async-done | bytes 98320 | tf_op jit(solution)/shard_map/psum | solution.py:134
  671.2 26.0 %all-reduce.156.cloned.1.call-done = (bf16[12,64,64]{2,1,0:T(8,128)(2,1)}, bf16[12,64,64]{1,2,0:T(8,128)(2,1)}) async-done(((bf16[12,64,64]{2,1,0:T(8,128)(2,1)}, bf16[12,64,64]{1,2,0:T(8,128)(2,1)}), (bf16[12,64,64]{2,1,0:T(8,128)(2,1)}, bf16[12,64,64]{1,2,0:T(8,128)(2,1)})) %all-reduce.156.cloned.1.call-update) | async-done | bytes 196624 | tf_op jit(solution)/shard_map/psum | solution.py:133
  705.2 3.5 all-to-all-start.7
  712.3 7.4 all-to-all-done.7
  724.5 3.5 fusion
  728.0 2.6 fusion.2
  734.7 6.6 all_gather.66
  745.5 5.0 all-reduce.137
  750.5 7.4 all-reduce.134
  758.0 61.5 %all-reduce.135 = (bf16[1,12,33]{2,1,0:T(8,128)(2,1)S(1)}, bf16[1,12,33]{2,1,0:T(8,128)(2,1)S(1)}, bf16[1,2,768]{2,1,0:T(2,128)(2,1)S(1)}, bf16[1,2,768]{2,1,0:T...) all-reduce(bf16[1,12,33]{2,1,0:T(8,128)(2,1)S(1)} %bitcast.791, ...), channel_id=1, replica_groups=mesh['dp'=16,'mp'=2] {'dp'}, use_global_device_ids=true, to_apply=%region_136.137 | all-reduce | flops 6936 | bytes 27744 | tf_op jit(solution)/shard_map/psum | solution.py:380
  822.3 6.3 all_gather.71
  829.6 176.7 %all-reduce.154.cloned.1.call-done = (bf16[1,768,3,384]{1,3,2,0:T(8,128)(2,1)}, bf16[1,768,3,384]{1,3,2,0:T(8,128)(2,1)}, bf16[1,384,768]{2,1,0:T(8,128)(2,1)}, ...) async-done(((bf16[1,768,3,384]{1,3,2,0:T(8,128)(2,1)}, ...) | async-done | bytes 14155792 | tf_op jit(solution)/shard_map/psum | solution.py:379
  1006.2 5.4 maximum_convert_fusion.2
  1011.7 8.1 copy.278
  1022.3 6.2 maximum_convert_fusion
  1028.5 4.4 maximum_convert_fusion.1
  (1252 shorter events, 295.0 us)
Async XLA Ops:
  10.9 15.8 %all-to-all-start = ((bf16[256,3,384]{2,1,0:T(4,128)(2,1)}), bf16[256,3,384]{2,1,0:T(4,128)(2,1)S(1)}, u32[]{:S(2)}, u32[]{:S(2)}) async-start(bf16[256,3,384]{2,1,0:T(4,128)(2,1)} %copy.173), calls=%async_computation | async-start | bytes 1572864 | tf_op jit(solution)/shard_map/all_to_all | solution.py:259
  15.1 41.0 %all-reduce.162.cloned.1.call-start = ((), (), s32[]{:S(2)}) async-start(), calls=%async_computation.30 | async-start | bytes 786432 | tf_op jit(solution)/shard_map/psum | solution.py:107
  15.8 91.3 %copy-start.217 = (f32[256]{0:T(256)}, f32[256]{0:T(256)S(1)}, u32[]{:S(2)}) copy-start(f32[256]{0:T(256)S(1)} %fusion.456) | copy-start | bytes 3076
  17.0 179.1 %copy-start.219 = (f32[64]{0:T(128)}, f32[64]{0:T(128)S(1)}, u32[]{:S(2)}) copy-start(f32[64]{0:T(128)S(1)} %fusion.416) | copy-start | bytes 772
  17.7 40.2 %copy-start.227 = (pred[128]{0:T(512)(128)(4,1)}, pred[128]{0:T(512)(128)(4,1)S(1)}, u32[]{:S(2)}) copy-start(pred[128]{0:T(512)(128)(4,1)S(1)} %get-tuple-element.292) | copy-start | bytes 388
  27.3 31.3 %copy-start.12 = (bf16[2,128,3,384]{1,3,0,2:T(8,128)(2,1)}, bf16[2,128,3,384]{1,3,0,2:T(8,128)(2,1)S(1)}, u32[]{:S(2)}) copy-start(bf16[2,128,3,384]{1,3,0,2:T(8,128)(2,1)S(1)} %copy.174) | copy-start | bytes 1769476
  58.6 34.2 %copy-start.16 = (f32[12,64,64]{1,2,0:T(8,128)}, f32[12,64,64]{1,2,0:T(8,128)S(1)}, u32[]{:S(2)}) copy-start(f32[12,64,64]{1,2,0:T(8,128)S(1)} %get-tuple-element.382) | copy-start | bytes 589828
  58.9 38.1 %copy-start.25 = (f32[12,128,64]{1,2,0:T(8,128)}, f32[12,128,64]{1,2,0:T(8,128)S(1)}, u32[]{:S(2)}) copy-start(f32[12,128,64]{1,2,0:T(8,128)S(1)} %get-tuple-element.386) | copy-start | bytes 1179652
  98.8 20.6 %copy-start.317 = (f32[2,2,768]{2,1,0:T(2,128)S(1)}, f32[2,2,768]{2,1,0:T(2,128)}, u32[]{:S(2)}) copy-start(f32[2,2,768]{2,1,0:T(2,128)} %param.16) | copy-start | bytes 36868
  98.8 33.8 %copy-start.47 = (bf16[256,768]{1,0:T(8,128)(2,1)S(1)}, bf16[256,768]{1,0:T(8,128)(2,1)}, u32[]{:S(2)}) copy-start(bf16[256,768]{1,0:T(8,128)(2,1)} %param.10) | copy-start | bytes 1179652
  98.8 8.4 all-to-all-start.1
  102.3 30.2 %reduce-scatter.9.cloned.1.call-start = ((), (), s32[]{:S(2)}) async-start(), calls=%async_computation.16 | async-start | bytes 589824 | tf_op jit(solution)/shard_map/reduce_scatter | solution.py:226
  103.5 31.3 %copy-start.275 = (f32[384]{0:T(512)}, f32[384]{0:T(512)S(1)}, u32[]{:S(2)}) copy-start(f32[384]{0:T(512)S(1)} %get-tuple-element.221) | copy-start | bytes 4612
  103.5 31.3 %copy-start.277 = (f32[384]{0:T(512)}, f32[384]{0:T(512)S(1)}, u32[]{:S(2)}) copy-start(f32[384]{0:T(512)S(1)} %get-tuple-element.222) | copy-start | bytes 4612
  103.5 31.3 %copy-start.279 = (f32[384]{0:T(512)}, f32[384]{0:T(512)S(1)}, u32[]{:S(2)}) copy-start(f32[384]{0:T(512)S(1)} %get-tuple-element.223) | copy-start | bytes 4612
  103.5 31.3 %copy-start.281 = (f32[384]{0:T(512)}, f32[384]{0:T(512)S(1)}, u32[]{:S(2)}) copy-start(f32[384]{0:T(512)S(1)} %get-tuple-element.224) | copy-start | bytes 4612
  103.5 31.3 %copy-start.283 = (f32[384]{0:T(512)}, f32[384]{0:T(512)S(1)}, u32[]{:S(2)}) copy-start(f32[384]{0:T(512)S(1)} %get-tuple-element.225) | copy-start | bytes 4612
  103.5 31.3 %copy-start.285 = (f32[384]{0:T(512)}, f32[384]{0:T(512)S(1)}, u32[]{:S(2)}) copy-start(f32[384]{0:T(512)S(1)} %get-tuple-element.226) | copy-start | bytes 4612
  103.5 31.3 %copy-start.287 = (f32[384]{0:T(512)}, f32[384]{0:T(512)S(1)}, u32[]{:S(2)}) copy-start(f32[384]{0:T(512)S(1)} %get-tuple-element.227) | copy-start | bytes 4612
  103.5 31.3 %copy-start.289 = (f32[384]{0:T(512)}, f32[384]{0:T(512)S(1)}, u32[]{:S(2)}) copy-start(f32[384]{0:T(512)S(1)} %get-tuple-element.228) | copy-start | bytes 4612
  103.5 31.3 %copy-start.291 = (f32[384]{0:T(512)}, f32[384]{0:T(512)S(1)}, u32[]{:S(2)}) copy-start(f32[384]{0:T(512)S(1)} %get-tuple-element.229) | copy-start | bytes 4612
  103.5 31.3 %copy-start.293 = (f32[384]{0:T(512)}, f32[384]{0:T(512)S(1)}, u32[]{:S(2)}) copy-start(f32[384]{0:T(512)S(1)} %get-tuple-element.230) | copy-start | bytes 4612
  103.6 31.3 %copy-start.294 = (f32[384]{0:T(512)}, f32[384]{0:T(512)S(1)}, u32[]{:S(2)}) copy-start(f32[384]{0:T(512)S(1)} %get-tuple-element.231) | copy-start | bytes 4612
  117.0 26.3 %copy-start.126 = (bf16[256,384]{1,0:T(8,128)(2,1)}, bf16[256,384]{1,0:T(8,128)(2,1)S(1)}, u32[]{:S(2)}) copy-start(bf16[256,384]{1,0:T(8,128)(2,1)S(1)} %fusion.179) | copy-start | bytes 589828
  119.3 44.5 %reduce-scatter.11.cloned.1.call-start = ((), (), s32[]{:S(2)}) async-start(), calls=%async_computation.17 | async-start | bytes 589824 | tf_op jit(solution)/shard_map/reduce_scatter | solution.py:226
  120.0 25.8 %copy-start.212 = (f32[768]{0:T(1024)}, f32[768]{0:T(1024)S(1)}, u32[]{:S(2)}) copy-start(f32[768]{0:T(1024)S(1)} %get-tuple-element.414) | copy-start | bytes 9220
  120.0 46.0 %copy-start.214 = (f32[768]{0:T(1024)}, f32[768]{0:T(1024)S(1)}, u32[]{:S(2)}) copy-start(f32[768]{0:T(1024)S(1)} %get-tuple-element.413) | copy-start | bytes 9220
  143.2 22.8 %copy-start.8 = (bf16[256,768]{1,0:T(8,128)(2,1)}, bf16[256,768]{1,0:T(8,128)(2,1)S(1)}, u32[]{:S(2)}) copy-start(bf16[256,768]{1,0:T(8,128)(2,1)S(1)} %all_gather.59) | copy-start | bytes 1179652
  178.9 13.7 %all-to-all-start.2 = ((bf16[256,3,384]{2,1,0:T(4,128)(2,1)}), bf16[256,3,384]{2,1,0:T(4,128)(2,1)S(1)}, u32[]{:S(2)}, u32[]{:S(2)}) async-start(bf16[256,3,384]{2,1,0:T(4,128)(2,1)} %copy.191), calls=%async_computation.4 | async-start | bytes 1572864 | tf_op jit(solution)/shard_map/all_to_all | solution.py:259
  182.5 40.8 %copy-start.228 = (pred[128]{0:T(512)(128)(4,1)S(1)}, pred[128]{0:T(512)(128)(4,1)}, u32[]{:S(2)}) copy-start(pred[128]{0:T(512)(128)(4,1)} %copy-done.227) | copy-start | bytes 388
  182.5 40.8 %all-reduce.160.cloned.1.call-start = ((), (), s32[]{:S(2)}) async-start(), calls=%async_computation.29 | async-start | bytes 786432 | tf_op jit(solution)/shard_map/psum | solution.py:107
  195.1 30.8 %copy-start.14 = (bf16[2,128,3,384]{1,3,0,2:T(8,128)(2,1)}, bf16[2,128,3,384]{1,3,0,2:T(8,128)(2,1)S(1)}, u32[]{:S(2)}) copy-start(bf16[2,128,3,384]{1,3,0,2:T(8,128)(2,1)S(1)} %copy.192) | copy-start | bytes 1769476
  225.9 21.5 %copy-start.21 = (f32[12,64,64]{1,2,0:T(8,128)}, f32[12,64,64]{1,2,0:T(8,128)S(1)}, u32[]{:S(2)}) copy-start(f32[12,64,64]{1,2,0:T(8,128)S(1)} %get-tuple-element.388) | copy-start | bytes 589828
  268.9 8.2 all-to-all-start.3
  272.3 32.2 %reduce-scatter.13.cloned.1.call-start = ((), (), s32[]{:S(2)}) async-start(), calls=%async_computation.18 | async-start | bytes 589824 | tf_op jit(solution)/shard_map/reduce_scatter | solution.py:226
  277.2 29.6 %copy-start.216 = (f32[768]{0:T(1024)S(1)}, f32[768]{0:T(1024)}, u32[]{:S(2)}) copy-start(f32[768]{0:T(1024)} %get-tuple-element.411) | copy-start | bytes 9220
  291.2 45.3 %reduce-scatter.15.cloned.1.call-start = ((), (), s32[]{:S(2)}) async-start(), calls=%async_computation.19 | async-start | bytes 589824 | tf_op jit(solution)/shard_map/reduce_scatter | solution.py:226
  323.2 46.6 %reduce-scatter.17.cloned.1.call-start = ((), (), s32[]{:S(2)}) async-start(), calls=%async_computation.20 | async-start | bytes 589824 | tf_op jit(solution)/shard_map/reduce_scatter | solution.py:226
  385.2 8.2 all-to-all-start.4
  388.6 33.4 %all-reduce.150.cloned.1.call-start = ((), (), s32[]{:S(2)}) async-start(), calls=%async_computation.21 | async-start | bytes 393216 | tf_op jit(solution)/shard_map/psum | solution.py:134
  396.4 25.6 %copy-start.339 = (f32[12,64]{1,0:T(8,128)S(1)}, f32[12,64]{1,0:T(8,128)}, u32[]{:S(2)}) copy-start(f32[12,64]{1,0:T(8,128)} %copy-done.338) | copy-start | bytes 9220
  396.4 25.6 %copy-start.342 = (f32[12,64]{1,0:T(8,128)S(1)}, f32[12,64]{1,0:T(8,128)}, u32[]{:S(2)}) copy-start(f32[12,64]{1,0:T(8,128)} %copy-done.341) | copy-start | bytes 9220
  396.4 25.6 %copy-start.345 = (f32[12,64]{1,0:T(8,128)S(1)}, f32[12,64]{1,0:T(8,128)}, u32[]{:S(2)}) copy-start(f32[12,64]{1,0:T(8,128)} %copy-done.344) | copy-start | bytes 9220
  398.8 24.8 %copy-start.179 = (pred[12,128,64]{1,2,0:T(32,128)(4,1)}, pred[12,128,64]{1,2,0:T(32,128)(4,1)S(1)}, u32[]{:S(2)}) copy-start(pred[12,128,64]{1,2,0:T(32,128)(4,1)S(1)} %get-tuple-element.287) | copy-start | bytes 294916
  398.8 95.8 %all-reduce.158.cloned.1.call-start = ((), (), s32[]{:S(2)}) async-start(), calls=%async_computation.28 | async-start | bytes 786432 | tf_op jit(solution)/shard_map/psum | solution.py:133
  465.2 29.4 %copy-start.119 = (bf16[12,64,64]{1,2,0:T(8,128)(2,1)S(1)}, bf16[12,64,64]{1,2,0:T(8,128)(2,1)}, u32[]{:S(2)}) copy-start(bf16[12,64,64]{1,2,0:T(8,128)(2,1)} %get-tuple-element.264) | copy-start | bytes 294916
  468.5 29.8 %copy-start.220 = (f32[64]{0:T(128)S(1)}, f32[64]{0:T(128)}, u32[]{:S(2)}) copy-start(f32[64]{0:T(128)} %copy-done.219) | copy-start | bytes 772
  505.1 15.5 %all-to-all-start.5 = ((bf16[128,3,768]{0,1,2:T(4,128)(2,1)}), bf16[128,3,768]{0,1,2:T(4,128)(2,1)}, u32[]{:S(2)}, u32[]{:S(2)}) async-start(bf16[128,3,768]{0,1,2:T(4,128)(2,1)} %pad_maximum_fusion), calls=%async_computation.10 | async-start | bytes 1572864 | tf_op jit(solution)/shard_map/all_to_all | solution.py:359
  509.4 32.2 %reduce-scatter.19.cloned.1.call-start = ((), (), s32[]{:S(2)}) async-start(), calls=%async_computation.22 | async-start | bytes 589824 | tf_op jit(solution)/shard_map/reduce_scatter | solution.py:226
  528.3 45.9 %reduce-scatter.21.cloned.1.call-start = ((), (), s32[]{:S(2)}) async-start(), calls=%async_computation.23 | async-start | bytes 589824 | tf_op jit(solution)/shard_map/reduce_scatter | solution.py:226
  589.5 8.2 all-to-all-start.6
  593.0 33.5 %all-reduce.152.cloned.1.call-start = ((), (), s32[]{:S(2)}) async-start(), calls=%async_computation.24 | async-start | bytes 393216 | tf_op jit(solution)/shard_map/psum | solution.py:134
  600.6 25.9 %copy-start.332 = (f32[12,64]{1,0:T(8,128)S(1)}, f32[12,64]{1,0:T(8,128)}, u32[]{:S(2)}) copy-start(f32[12,64]{1,0:T(8,128)} %copy-done.331) | copy-start | bytes 9220
  600.6 25.9 %copy-start.334 = (f32[12,64]{1,0:T(8,128)S(1)}, f32[12,64]{1,0:T(8,128)}, u32[]{:S(2)}) copy-start(f32[12,64]{1,0:T(8,128)} %copy-done.333) | copy-start | bytes 9220
  600.6 25.9 %copy-start.336 = (f32[12,64]{1,0:T(8,128)S(1)}, f32[12,64]{1,0:T(8,128)}, u32[]{:S(2)}) copy-start(f32[12,64]{1,0:T(8,128)} %copy-done.335) | copy-start | bytes 9220
  603.1 94.2 %all-reduce.156.cloned.1.call-start = ((), (), s32[]{:S(2)}) async-start(), calls=%async_computation.27 | async-start | bytes 786432 | tf_op jit(solution)/shard_map/psum | solution.py:133
  668.9 28.4 %copy-start.115 = (bf16[12,64,64]{1,2,0:T(8,128)(2,1)S(1)}, bf16[12,64,64]{1,2,0:T(8,128)(2,1)}, u32[]{:S(2)}) copy-start(bf16[12,64,64]{1,2,0:T(8,128)(2,1)} %get-tuple-element.266) | copy-start | bytes 294916
  668.9 28.4 %copy-start.181 = (pred[12,64,64]{1,2,0:T(32,128)(4,1)S(1)}, pred[12,64,64]{1,2,0:T(32,128)(4,1)}, u32[]{:S(2)}) copy-start(pred[12,64,64]{1,2,0:T(32,128)(4,1)} %get-tuple-element.271) | copy-start | bytes 147460
  671.1 27.7 %copy-start.117 = (bf16[12,64,64]{1,2,0:T(8,128)(2,1)S(1)}, bf16[12,64,64]{1,2,0:T(8,128)(2,1)}, u32[]{:S(2)}) copy-start(bf16[12,64,64]{1,2,0:T(8,128)(2,1)} %get-tuple-element.267) | copy-start | bytes 294916
  671.1 27.7 %copy-start.182 = (pred[12,64,64]{1,2,0:T(32,128)(4,1)S(1)}, pred[12,64,64]{1,2,0:T(32,128)(4,1)}, u32[]{:S(2)}) copy-start(pred[12,64,64]{1,2,0:T(32,128)(4,1)} %get-tuple-element.271) | copy-start | bytes 147460
  705.2 14.6 %all-to-all-start.7 = ((bf16[128,3,768]{0,1,2:T(4,128)(2,1)}), bf16[128,3,768]{0,1,2:T(4,128)(2,1)S(1)}, u32[]{:S(2)}, u32[]{:S(2)}) async-start(bf16[128,3,768]{0,1,2:T(4,128)(2,1)} %pad_maximum_fusion.1), calls=%async_computation.14 | async-start | bytes 1572864 | tf_op jit(solution)/shard_map/all_to_all | solution.py:359
  708.7 112.6 %reduce-scatter.23.cloned.1.call-start = ((), (), s32[]{:S(2)}) async-start(), calls=%async_computation.25 | async-start | bytes 589824 | tf_op jit(solution)/shard_map/reduce_scatter | solution.py:226
  724.3 282.0 %all-reduce.154.cloned.1.call-start = ((), (), s32[]{:S(2)}) async-start(), calls=%async_computation.26 | async-start | bytes 28311552 | tf_op jit(solution)/shard_map/psum | solution.py:379
  743.6 77.7 %copy-start.159 = (f32[128,768]{1,0:T(8,128)S(1)}, f32[128,768]{1,0:T(8,128)}, u32[]{:S(2)}) copy-start(f32[128,768]{1,0:T(8,128)} %get-tuple-element.277) | copy-start | bytes 1179652
  (361 other events, 1698.2 us)
Sparse Core Ops, SparseCore 0:
  29.6 26.4 all-reduce.161
  119.4 13.1 reduce-scatter.8
  150.6 13.1 reduce-scatter.10
  197.4 25.8 all-reduce.159
  291.3 13.1 reduce-scatter.12
  323.3 13.1 reduce-scatter.14
  356.6 13.1 reduce-scatter.16
  398.9 23.0 all-reduce.149
  468.7 25.8 all-reduce.157
  528.5 13.1 reduce-scatter.18
  561.1 13.1 reduce-scatter.20
  603.2 23.2 all-reduce.151
  671.3 25.9 all-reduce.155
  724.4 13.1 reduce-scatter.22
  743.8 262.3 all-reduce.153
where the time goes:
time: 1050 us; the launch traced here: 1040 us
  waiting for transfers between devices  439 us (42%)
  matrix products  214 us (20%)
  blocking collectives  169 us (16%)
  other arithmetic  107 us (10%)
  local copies, waits for them, and re-layouts  57.2 us (5%)
  starting transfers between devices  30.8 us (3%)
  between operations  22 us (2%)
    psum x1, waiting for transfers between devices, sum_layer(): lax.psum(parts[0].astype(jnp.bfloat16), 'dp').astype(jnp.float32)  177 us
    reduce_scatter x8, waiting for transfers between devices, row_sums(): lax.psum_scatter(partial_value.astype(jnp.bfloat16), 'mp', scatter_dimens...  80.3 us
    all_gather x9, blocking collectives, whole_rows(): lax.all_gather(share.astype(jnp.bfloat16), 'mp', axis=0, tiled=True)  64.3 us
    psum x1, blocking collectives, sum_layer(): lax.psum(parts[1].astype(jnp.bfloat16), 'dp').astype(jnp.float32)  61.5 us
    psum x2, waiting for transfers between devices, attend_back(): lax.psum(kland_part.astype(jnp.bfloat16), 'mp').astype(jnp.float32)  52.1 us
    psum x2, waiting for transfers between devices, attend(): lax.psum(query_portion.astype(jnp.bfloat16), 'mp').astype(jnp.float32)  50.4 us
    psum x2, waiting for transfers between devices, attend_back(): lax.psum(carried_part.astype(jnp.bfloat16), 'mp').astype(jnp.float32)  37.8 us
    unnamed x810, local copies, waits for them, and re-layouts  36.5 us
  transfers between devices with their start and end apart: 23, of which 22 were waited for; matrix products, arithmetic and copies ran while one was open for 5% of the time, Pallas kernels for 0%

commit v1 on v0

--- a/solution.py
+++ b/solution.py
@@ -1,6 +1,10 @@
+import functools
+
 import jax
 import jax.numpy as jnp
 from jax import lax
+from jax.experimental import pallas as pl
+from jax.experimental.pallas import tpu as pltpu
 from jax.sharding import PartitionSpec as P
 
 M = 64
@@ -454,9 +458,610 @@
     )
 
 
+MESH = pl.DeviceIdType.MESH
+F32 = jnp.float32
+BF16 = jnp.bfloat16
+
+
+def nn(a, b):
+    return lax.dot_general(a, b, (((1,), (0,)), ((), ())), preferred_element_type=F32)
+
+
+def nt(a, b):
+    return lax.dot_general(a, b, (((1,), (1,)), ((), ())), preferred_element_type=F32)
+
+
+def parts_of(x):
+    high = x.astype(BF16)
+    return high, (x - high.astype(F32)).astype(BF16)
+
+
+def nn3(a, b):
+    return nn(jnp.concatenate([a[0], a[1]], 1), jnp.concatenate([b[0], b[0]], 0)) + nn(a[0], b[1])
+
+
+def nt3(a, b):
+    return nt(jnp.concatenate([a[0], a[1]], 1), jnp.concatenate([b[0], b[0]], 1)) + nt(a[0], b[1])
+
+
+def iota(shape, axis):
+    return lax.broadcasted_iota(jnp.int32, shape, axis)
+
+
+class Frame:
+    def __init__(self, length, rows, size_h):
+        self.length = length
+        self.rows = rows
+        self.lane0 = iota((1, 2 * size_h), 1) < size_h
+        self.keep = [self.lane0.astype(F32).astype(BF16), (~self.lane0).astype(F32).astype(BF16)]
+        self.diag = (iota((2 * M, 2 * M), 0) < M) == (iota((2 * M, 2 * M), 1) < M)
+        self.ones = self.diag.astype(F32).astype(BF16)
+        self.ones2 = jnp.concatenate([self.ones, self.ones], 0)
+        j, t = iota((M, rows), 0), iota((M, rows), 1)
+        member = (t * M >= j * length) & (t * M < (j + 1) * length)
+        member = member.astype(F32)
+        self.member = member.astype(BF16)
+        self.inv = 1.0 / jnp.sum(member, axis=1, keepdims=True)
+        t, j = iota((rows, M), 0), iota((rows, M), 1)
+        self.member_t = ((t * M >= j * length) & (t * M < (j + 1) * length)).astype(F32).astype(BF16)
+        self.valid = (iota((rows, 1), 0) < length).astype(F32)
+        self.valid_lane = iota((1, rows), 1) < length
+        self.band = jnp.abs(iota((rows, rows), 0) - iota((rows, rows), 1)) <= KREACH
+
+    def stack(self, x):
+        return jnp.where(self.diag, jnp.concatenate([x, x], 0), 0.0)
+
+    def block(self, x):
+        return jnp.where(self.diag, x, 0.0)
+
+    def half_sums(self, x):
+        high, low = parts_of(x)
+        return nn(jnp.concatenate([high, low], 1), self.ones2)
+
+    def toeplitz(self, row):
+        spread = jnp.broadcast_to(row, (self.rows, self.rows))
+        turned = pltpu.roll(spread, self.rows - KREACH, 1, stride=1, stride_axis=0)
+        return jnp.where(self.band, turned, 0.0).astype(BF16)
+
+    def conv(self, rows_pair, value):
+        both = jnp.concatenate([self.toeplitz(rows_pair[0]), self.toeplitz(rows_pair[1])], 1)
+        stacked = jnp.concatenate([value * self.keep[0], value * self.keep[1]], 0)
+        return nn(both, stacked)
+
+    def diagonals(self, product):
+        banded = jnp.where(self.band, product, 0.0)
+        total = banded[:8]
+        for group in range(1, self.rows // 8):
+            part = banded[8 * group : 8 * group + 8]
+            total = total + pltpu.roll(part, self.rows - 8 * group, 1)
+        total = pltpu.roll(total, KREACH, 1)
+        result = total[:1]
+        for row in range(1, 8):
+            result = result + pltpu.roll(total[row : row + 1], self.rows - row, 1)
+        return result
+
+
+KREACH = 16
+
+
+def softmax_masked(scores, live):
+    scores = jnp.where(live, scores, -1e30)
+    top = jnp.max(scores, axis=-1, keepdims=True)
+    powers = jnp.where(live, jnp.exp(scores - top), 0.0)
+    return powers / jnp.sum(powers, axis=-1, keepdims=True)
+
+
+def attention(frame, qkv, taps, head0, size_h, keep, out_ref):
+    scale = size_h ** (-0.5)
+    pairs = qkv.shape[2] // (2 * size_h)
+    ql = nn(frame.member, qkv[0]) * frame.inv
+    kl = nn(frame.member, qkv[1]) * frame.inv
+    keep["ql"][...] = ql
+    keep["kl"][...] = kl
+    cols = [slice(p * 2 * size_h, (p + 1) * 2 * size_h) for p in range(pairs)]
+    qs = [parts_of(frame.stack(ql[:, c])) for c in cols]
+    ks = [parts_of(frame.stack(kl[:, c])) for c in cols]
+    second = [softmax_masked(nt3(qs[p], ks[p]) * scale, frame.diag) for p in range(pairs)]
+    inverse = []
+    halves = iota((2 * M, 1), 0) < M
+    for p in range(pairs):
+        keep["second"][p] = second[p]
+        squares = jnp.sum(second[p] * second[p], axis=1, keepdims=True)
+        first_total = jnp.sum(jnp.where(halves, squares, 0.0), axis=0, keepdims=True)
+        other_total = jnp.sum(jnp.where(halves, 0.0, squares), axis=0, keepdims=True)
+        inverse.append(second[p].T * (1.0 / jnp.where(halves, first_total, other_total)))
+    second_parts = [parts_of(s) for s in second]
+    for sweep in range(NEWTON):
+        for p in range(pairs):
+            keep["inverse"][sweep, p] = inverse[p]
+        zp = [parts_of(z) for z in inverse]
+        product = [nn3(second_parts[p], zp[p]) for p in range(pairs)]
+        pp = [parts_of(x) for x in product]
+        square = [nn3(pp[p], pp[p]) for p in range(pairs)]
+        forward = [nn3(zp[p], pp[p]) for p in range(pairs)]
+        last = [
+            nn3(parts_of(forward[p]), parts_of(7.0 * product[p] - square[p])) for p in range(pairs)
+        ]
+        inverse = [
+            0.25 * (13.0 * inverse[p] - 15.0 * forward[p] + last[p]) for p in range(pairs)
+        ]
+    for p in range(pairs):
+        c = cols[p]
+        keep["inverse"][NEWTON, p] = inverse[p]
+        query, key, value = qkv[0, :, c], qkv[1, :, c], qkv[2, :, c]
+        scores = nt(jnp.concatenate([query, query], 1), jnp.concatenate(ks[p], 1)) * scale
+        top0 = jnp.max(jnp.where(frame.lane0, scores, -1e30), axis=-1, keepdims=True)
+        top1 = jnp.max(jnp.where(frame.lane0, -1e30, scores), axis=-1, keepdims=True)
+        powers = jnp.exp(scores - jnp.where(frame.lane0, top0, top1))
+        first = (powers / frame.half_sums(powers)).astype(BF16)
+        keep["first"][:, c] = first
+        scores = nt(jnp.concatenate(qs[p], 1), jnp.concatenate([key, key], 1)) * scale
+        third = softmax_masked(scores, frame.valid_lane).astype(BF16)
+        keep["third"][p] = third
+        summary = frame.block(nn(third, value))
+        keep["summary"][p] = summary
+        carried = nn3(parts_of(inverse[p]), parts_of(summary))
+        keep["carried"][p] = carried
+        mixed = nn(first, carried.astype(BF16))
+        inside = (value.astype(F32) * frame.valid).astype(BF16)
+        rows_pair = [taps[pl.ds(head0 + 2 * p + i, 1), :] for i in range(2)]
+        mixed = (mixed + frame.conv(rows_pair, inside)) * frame.valid
+        out_ref[:, c] = mixed.astype(BF16)
+
+
+def attention_back(frame, grad, qkv, taps_turned, head0, size_h, keep, out_ref, taps_out):
+    scale = size_h ** (-0.5)
+    pairs = qkv.shape[2] // (2 * size_h)
+    cols = [slice(p * 2 * size_h, (p + 1) * 2 * size_h) for p in range(pairs)]
+    each = range(pairs)
+    ql, kl = keep["ql"][...], keep["kl"][...]
+    qs = [parts_of(frame.stack(ql[:, c])) for c in cols]
+    ks = [parts_of(frame.stack(kl[:, c])) for c in cols]
+    summary = [keep["summary"][p] for p in each]
+    second = [keep["second"][p] for p in each]
+    dq, dk_landmark, dcarried, grad_low = [], [], [], []
+    for p in each:
+        c = cols[p]
+        g = grad[:, c].astype(BF16)
+        grad_low.append(g)
+        first = keep["first"][:, c].astype(F32)
+        dfirst = nt(g, keep["carried"][p].astype(BF16))
+        slope = first * dfirst
+        slope = (slope - first * frame.half_sums(slope)) * scale
+        dq.append(nn(slope.astype(BF16), ks[p][0]))
+        dk_landmark.append(frame.block(nn(slope.T.astype(BF16), qkv[0, :, c])))
+        dcarried.append(frame.block(nn(first.T.astype(BF16), g)))
+    dcp = [parts_of(x) for x in dcarried]
+    up = [nt3(dcp[p], parts_of(summary[p])) for p in each]
+    dsummary = [nn3(parts_of(keep["inverse"][NEWTON, p].T), dcp[p]) for p in each]
+    second_parts = [parts_of(s) for s in second]
+    second_turned = [parts_of(s.T) for s in second]
+    dsecond = [jnp.zeros_like(s) for s in second]
+    for sweep in reversed(range(NEWTON)):
+        inverse = [keep["inverse"][sweep, p] for p in each]
+        zp = [parts_of(z) for z in inverse]
+        product = [nn3(second_parts[p], zp[p]) for p in each]
+        pp = [parts_of(x) for x in product]
+        inner = [parts_of(7.0 * product[p] - nn3(pp[p], pp[p])) for p in each]
+        forward_turned = [parts_of(nn3(zp[p], pp[p]).T) for p in each]
+        product_turned = [parts_of(x.T) for x in product]
+        inverse_turned = [parts_of(z.T) for z in inverse]
+        upp = [parts_of(x) for x in up]
+        dforward = [parts_of(0.25 * (nt3(upp[p], inner[p]) - 15.0 * up[p])) for p in each]
+        dinner_full = [0.25 * nn3(forward_turned[p], upp[p]) for p in each]
+        dinner = [parts_of(x) for x in dinner_full]
+        dproduct = [
+            parts_of(
+                7.0 * dinner_full[p]
+                - nt3(dinner[p], pp[p])
+                - nn3(product_turned[p], dinner[p])
+                + nn3(inverse_turned[p], dforward[p])
+            )
+            for p in each
+        ]
+        up = [
+            3.25 * up[p] + nt3(dforward[p], pp[p]) + nn3(second_turned[p], dproduct[p])
+            for p in each
+        ]
+        dsecond = [dsecond[p] + nt3(dproduct[p], zp[p]) for p in each]
+    halves = iota((2 * M, 1), 0) < M
+    for p in each:
+        c = cols[p]
+        query, key, value = qkv[0, :, c], qkv[1, :, c], qkv[2, :, c]
+        squares = jnp.sum(second[p] * second[p], axis=1, keepdims=True)
+        total0 = jnp.sum(jnp.where(halves, squares, 0.0), axis=0, keepdims=True)
+        total1 = jnp.sum(jnp.where(halves, 0.0, squares), axis=0, keepdims=True)
+        inverse_total = 1.0 / jnp.where(halves, total0, total1)
+        start_agree = jnp.sum(up[p] * keep["inverse"][0, p], axis=1, keepdims=True)
+        agree0 = jnp.sum(jnp.where(halves, start_agree, 0.0), axis=0, keepdims=True)
+        agree1 = jnp.sum(jnp.where(halves, 0.0, start_agree), axis=0, keepdims=True)
+        agree = jnp.where(halves, agree0, agree1)
+        dsec = dsecond[p] + (up[p].T - 2.0 * agree * second[p]) * inverse_total
+        slope = second[p] * dsec
+        slope = (slope - second[p] * jnp.sum(slope, axis=-1, keepdims=True)) * scale
+        dql = nn(slope.astype(BF16), ks[p][0])
+        dkl = nn(slope.T.astype(BF16), qs[p][0]) + dk_landmark[p]
+        third = keep["third"][p].astype(F32)
+        ds = dsummary[p].astype(BF16)
+        dthird = nt(ds, value)
+        agreed = jnp.sum(dsummary[p] * summary[p], axis=-1, keepdims=True)
+        slope = third * (dthird - agreed) * scale
+        dv = nn(third.T.astype(BF16), ds)
+        dql = dql + frame.block(nn(slope.astype(BF16), key))
+        dk = nn(slope.T.astype(BF16), qs[p][0])
+        dql = ((dql[:M] + dql[M:]) * frame.inv).astype(BF16)
+        dkl = ((dkl[:M] + dkl[M:]) * frame.inv).astype(BF16)
+        out_ref[0, :, c] = (dq[p] + nn(frame.member_t, dql)).astype(BF16)
+        out_ref[1, :, c] = (dk + nn(frame.member_t, dkl)).astype(BF16)
+        inside = (value.astype(F32) * frame.valid).astype(BF16)
+        rows_pair = [taps_turned[pl.ds(head0 + 2 * p + i, 1), :] for i in range(2)]
+        dv = dv + frame.valid * frame.conv(rows_pair, grad_low[p])
+        out_ref[2, :, c] = dv.astype(BF16)
+        for i in range(2):
+            product = nt(grad_low[p] * frame.keep[i], inside)
+            taps_out(2 * p + i, frame.diagonals(product))
+
+
+def norm_rows(r, gain, shift):
+    centre = r - jnp.mean(r, axis=-1, keepdims=True)
+    spread = lax.rsqrt(jnp.mean(centre * centre, axis=-1, keepdims=True) + 1e-05)
+    normed = centre * spread
+    return normed * gain + shift, normed, spread
+
+
+def norm_rows_back(dy, normed, spread, gain):
+    scaled = dy * gain
+    result = spread * (
+        scaled
+        - jnp.mean(scaled, axis=-1, keepdims=True)
+        - normed * jnp.mean(scaled * normed, axis=-1, keepdims=True)
+    )
+    return (
+        result,
+        jnp.sum(dy * normed, axis=0, keepdims=True),
+        jnp.sum(dy, axis=0, keepdims=True),
+    )
+
+
+GELU_A = 0.7978845608028654
+GELU_B = 0.044715
+
+
+def gelu_both(u):
+    square = u * u
+    t = jnp.tanh(GELU_A * (u + GELU_B * u * square))
+    half = 0.5 * (1.0 + t)
+    slope = half + 0.5 * u * (1.0 - t * t) * (GELU_A + (3.0 * GELU_A * GELU_B) * square)
+    return u * half, slope
+
+
+def whole_step(
+    length_ref,
+    tokens_ref,
+    cotangent_ref,
+    taps_ref,
+    turned_ref,
+    gains_ref,
+    shifts_ref,
+    projection_hbm,
+    output_hbm,
+    up_hbm,
+    down_hbm,
+    activations_ref,
+    token_grad_ref,
+    small_ref,
+    down_grad_hbm,
+    up_grad_hbm,
+    other_grad_hbm,
+    weights,
+    kept,
+    work,
+    grads,
+    wire,
+    sems,
+):
+    rows, width = tokens_ref.shape
+    columns = projection_hbm.shape[3]
+    hidden = up_hbm.shape[2]
+    heads = taps_ref.shape[1]
+    size_h = width // heads
+    half = rows // 2
+    tile = 384
+    dp, mp = lax.axis_index("dp"), lax.axis_index("mp")
+    head0 = mp * (columns // size_h)
+    partner = (dp, 1 - mp)
+
+    loads = []
+    order = [(projection_hbm, "projection"), (output_hbm, "output"), (up_hbm, "up"), (down_hbm, "down")]
+    for layer in range(LAYERS):
+        for index, (source, name) in enumerate(order):
+            load = pltpu.make_async_copy(
+                source.at[layer], weights[name].at[layer], sems["load"].at[layer * 4 + index]
+            )
+            load.start()
+            loads.append(load)
+
+    barrier = pltpu.get_barrier_semaphore()
+    pl.semaphore_signal(barrier, inc=1, device_id=partner, device_id_type=MESH)
+    pl.semaphore_wait(barrier, 1)
+
+    frame = Frame(length_ref[0], rows, size_h)
+    flights = {}
+
+    def send(slot, piece, partial_value):
+        span = pl.ds(piece * half, half)
+        wire["send"][slot % 2, span, :] = partial_value.astype(BF16)
+        copy = pltpu.make_async_remote_copy(
+            src_ref=wire["send"].at[slot % 2, span],
+            dst_ref=wire["receive"].at[slot, span],
+            send_sem=sems["send"].at[slot * 2 + piece],
+            recv_sem=sems["receive"].at[slot * 2 + piece],
+            device_id=partner,
+            device_id_type=MESH,
+        )
+        copy.start()
+        flights[slot, piece] = copy
+
+    def arrived(slot, piece):
+        span = pl.ds(piece * half, half)
+        flights[slot, piece].wait()
+        return wire["send"][slot % 2, span, :].astype(F32) + wire["receive"][
+            slot, span, :
+        ].astype(F32)
+
+    pieces = [slice(0, half), slice(half, rows)]
+    valid = [frame.valid[c] for c in pieces]
+
+    def project(layer, piece):
+        c = pieces[piece]
+        for i in range(3):
+            kept["qkv"][layer, i, c, :] = nn(
+                work["x_low"][c, :], weights["projection"][layer, i]
+            ).astype(BF16)
+
+    def keep_of(layer):
+        names = ("ql", "kl", "second", "inverse", "first", "third", "summary", "carried")
+        return {name: kept[name].at[layer] for name in names}
+
+    work["x"][...] = tokens_ref[...].astype(F32)
+    work["x_low"][...] = tokens_ref[...]
+    loads[0].wait()
+    for piece in range(2):
+        project(0, piece)
+    for layer in range(LAYERS):
+        attention(
+            frame,
+            kept["qkv"].at[layer],
+            taps_ref.at[layer],
+            head0,
+            size_h,
+            keep_of(layer),
+            work["mixed"],
+        )
+        loads[layer * 4 + 1].wait()
+        slot = layer * 2
+        for piece, c in enumerate(pieces):
+            send(slot, piece, nn(work["mixed"][c, :], weights["output"][layer]))
+        kept["mixed_t"][layer] = work["mixed"][...].T
+        kept["x_t"][layer] = work["x_low"][...].T
+        loads[layer * 4 + 2].wait()
+        loads[layer * 4 + 3].wait()
+        for piece, c in enumerate(pieces):
+            summed = work["x"][c, :] + arrived(slot, piece)
+            y, normed, spread = norm_rows(summed, gains_ref[layer, 0:1], shifts_ref[layer, 0:1])
+            kept["normed"][layer, 0, c, :] = normed
+            kept["spread"][layer, 0, c, :] = spread
+            work["y"][c, :] = y
+            work["y_low"][c, :] = y.astype(BF16)
+            for j in range(hidden // tile):
+                span = slice(j * tile, (j + 1) * tile)
+                u = nn(work["y_low"][c, :], weights["up"][layer, :, span])
+                active, slope = gelu_both(u)
+                work["active"][c, span] = active.astype(BF16)
+                kept["slope"][layer, c, span] = slope
+            send(slot + 1, piece, nn(work["active"][c, :], weights["down"][layer]))
+        kept["active_t"][layer] = work["active"][...].T
+        kept["y_t"][layer] = work["y_low"][...].T
+        if layer + 1 < LAYERS:
+            loads[layer * 4 + 4].wait()
+        for piece, c in enumerate(pieces):
+            summed = work["y"][c, :] + arrived(slot + 1, piece)
+            y, normed, spread = norm_rows(summed, gains_ref[layer, 1:2], shifts_ref[layer, 1:2])
+            kept["normed"][layer, 1, c, :] = normed
+            kept["spread"][layer, 1, c, :] = spread
+            if layer + 1 < LAYERS:
+                work["x"][c, :] = y
+                work["x_low"][c, :] = y.astype(BF16)
+                project(layer + 1, piece)
+            else:
+                activations_ref[c, :] = (y * valid[piece]).astype(BF16)
+
+    stores = []
+
+    def store(source, target, index):
+        copy = pltpu.make_async_copy(source, target, sems["store"].at[index])
+        copy.start()
+        stores.append(copy)
+
+    small_ref[...] = jnp.zeros_like(small_ref)
+    for piece, c in enumerate(pieces):
+        work["dy"][c, :] = cotangent_ref[c, :].astype(F32) * valid[piece]
+
+    def norm_back(layer, which):
+        gain = gains_ref[layer, which : which + 1]
+        gain_sum = shift_sum = 0.0
+        for c in pieces:
+            result, gain_part, shift_part = norm_rows_back(
+                work["dy"][c, :], kept["normed"][layer, which, c, :], kept["spread"][layer, which, c, :], gain
+            )
+            work["dr"][c, :] = result
+            work["e"][c, :] = result.astype(BF16)
+            gain_sum, shift_sum = gain_sum + gain_part, shift_sum + shift_part
+        row = layer * 2 + which
+        small_ref[row : row + 1, :] = gain_sum
+        small_ref[row + 4 : row + 5, :] = shift_sum
+
+    for layer in reversed(range(LAYERS)):
+        slot = 4 + (LAYERS - 1 - layer) * 2
+        norm_back(layer, 1)
+        for j in range(hidden // tile):
+            span = slice(j * tile, (j + 1) * tile)
+            grads["down"][layer, span, :] = nn(kept["active_t"][layer, span, :], work["e"][...]).astype(BF16)
+        store(grads["down"].at[layer], down_grad_hbm.at[layer], layer * 3)
+        for j in range(hidden // tile):
+            span = slice(j * tile, (j + 1) * tile)
+            dh = nt(work["e"][...], weights["down"][layer, span, :])
+            work["du"][:, span] = (dh * kept["slope"][layer, :, span]).astype(BF16)
+        for piece, c in enumerate(pieces):
+            send(slot, piece, nt(work["du"][c, :], weights["up"][layer]))
+        for j in range(hidden // tile):
+            span = slice(j * tile, (j + 1) * tile)
+            grads["up"][layer, :, span] = nn(kept["y_t"][layer], work["du"][:, span]).astype(BF16)
+        store(grads["up"].at[layer], up_grad_hbm.at[layer], layer * 3 + 1)
+        for piece, c in enumerate(pieces):
+            work["dy"][c, :] = work["dr"][c, :] + arrived(slot, piece)
+        norm_back(layer, 0)
+        for piece, c in enumerate(pieces):
+            work["dmixed"][c, :] = nt(work["e"][c, :], weights["output"][layer]) * valid[piece]
+        for j in range(2):
+            span = slice(j * columns, (j + 1) * columns)
+            grads["other"][layer, 0, span, :] = nn(kept["mixed_t"][layer], work["e"][:, span]).astype(BF16)
+
+        def taps_out(head, row, layer=layer):
+            small_ref[pl.ds(8 + layer * heads + head0 + head, 1), :rows] = row
+
+        attention_back(
+            frame,
+            work["dmixed"],
+            kept["qkv"].at[layer],
+            turned_ref.at[layer],
+            head0,
+            size_h,
+            keep_of(layer),
+            work["dqkv"],
+            taps_out,
+        )
+        for piece, c in enumerate(pieces):
+            total = 0.0
+            for i in range(3):
+                total = total + nt(work["dqkv"][i, c, :], weights["projection"][layer, i])
+            send(slot + 1, piece, total)
+        for i in range(3):
+            grads["other"][layer, 1 + i] = nn(kept["x_t"][layer], work["dqkv"][i]).astype(BF16)
+        store(grads["other"].at[layer], other_grad_hbm.at[layer], layer * 3 + 2)
+        target = work["dy"] if layer > 0 else token_grad_ref
+        for piece, c in enumerate(pieces):
+            target[c, :] = work["dr"][c, :] + arrived(slot + 1, piece)
+    for copy in stores:
+        copy.wait()
+
+
+def fused_body(tokens, lengths, cotangent, projection, conv_taps, output_weight, norm_gains, norm_shifts, up_weight, down_weight):
+    rows, width = tokens.shape
+    columns, hidden = projection.shape[3], up_weight.shape[2]
+    heads, reach = conv_taps.shape[1:]
+    size_h = width // heads
+    pairs = columns // (2 * size_h)
+    by_kind = jnp.transpose(projection, (0, 2, 1, 3))
+    room = ((0, 0), (0, 0), (0, rows - reach))
+    taps = jnp.pad(conv_taps, room)
+    turned = jnp.pad(conv_taps[:, :, ::-1], room)
+    vmem = pl.BlockSpec(memory_space=pltpu.VMEM)
+    hbm = pl.BlockSpec(memory_space=pl.ANY)
+    two = 2 * M
+    scratch = (
+        dict(
+            projection=pltpu.VMEM((LAYERS, 3, width, columns), BF16),
+            output=pltpu.VMEM((LAYERS, columns, width), BF16),
+            up=pltpu.VMEM((LAYERS, width, hidden), BF16),
+            down=pltpu.VMEM((LAYERS, hidden, width), BF16),
+        ),
+        dict(
+            qkv=pltpu.VMEM((LAYERS, 3, rows, columns), BF16),
+            ql=pltpu.VMEM((LAYERS, M, columns), F32),
+            kl=pltpu.VMEM((LAYERS, M, columns), F32),
+            second=pltpu.VMEM((LAYERS, pairs, two, two), F32),
+            inverse=pltpu.VMEM((LAYERS, NEWTON + 1, pairs, two, two), F32),
+            first=pltpu.VMEM((LAYERS, rows, columns), BF16),
+            third=pltpu.VMEM((LAYERS, pairs, two, rows), BF16),
+            summary=pltpu.VMEM((LAYERS, pairs, two, two), F32),
+            carried=pltpu.VMEM((LAYERS, pairs, two, two), F32),
+            normed=pltpu.VMEM((LAYERS, 2, rows, width), F32),
+            spread=pltpu.VMEM((LAYERS, 2, rows, 1), F32),
+            slope=pltpu.VMEM((LAYERS, rows, hidden), F32),
+            x_t=pltpu.VMEM((LAYERS, width, rows), BF16),
+            mixed_t=pltpu.VMEM((LAYERS, columns, rows), BF16),
+            y_t=pltpu.VMEM((LAYERS, width, rows), BF16),
+            active_t=pltpu.VMEM((LAYERS, hidden, rows), BF16),
+        ),
+        dict(
+            x=pltpu.VMEM((rows, width), F32),
+            x_low=pltpu.VMEM((rows, width), BF16),
+            y=pltpu.VMEM((rows, width), F32),
+            y_low=pltpu.VMEM((rows, width), BF16),
+            mixed=pltpu.VMEM((rows, columns), BF16),
+            active=pltpu.VMEM((rows, hidden), BF16),
+            dy=pltpu.VMEM((rows, width), F32),
+            dr=pltpu.VMEM((rows, width), F32),
+            e=pltpu.VMEM((rows, width), BF16),
+            du=pltpu.VMEM((rows, hidden), BF16),
+            dmixed=pltpu.VMEM((rows, columns), F32),
+            dqkv=pltpu.VMEM((3, rows, columns), BF16),
+        ),
+        dict(
+            down=pltpu.VMEM((LAYERS, hidden, width), BF16),
+            up=pltpu.VMEM((LAYERS, width, hidden), BF16),
+            other=pltpu.VMEM((LAYERS, 4, width, columns), BF16),
+        ),
+        dict(
+            send=pltpu.VMEM((2, rows, width), BF16),
+            receive=pltpu.VMEM((4 * LAYERS, rows, width), BF16),
+        ),
+        dict(
+            load=pltpu.SemaphoreType.DMA((4 * LAYERS,)),
+            store=pltpu.SemaphoreType.DMA((3 * LAYERS,)),
+            send=pltpu.SemaphoreType.DMA((8 * LAYERS,)),
+            receive=pltpu.SemaphoreType.DMA((8 * LAYERS,)),
+        ),
+    )
+    shape = jax.ShapeDtypeStruct
+    activations, token_grad, small, down_grad, up_grad, other_grad = pl.pallas_call(
+        whole_step,
+        out_shape=[
+            shape((rows, width), BF16),
+            shape((rows, width), F32),
+            shape((8 + LAYERS * heads, width), F32),
+            shape((LAYERS, hidden, width), BF16),
+            shape((LAYERS, width, hidden), BF16),
+            shape((LAYERS, 4, width, columns), BF16),
+        ],
+        in_specs=[pl.BlockSpec(memory_space=pltpu.SMEM)] + [vmem] * 6 + [hbm] * 4,
+        out_specs=[vmem] * 3 + [hbm] * 3,
+        scratch_shapes=scratch,
+        compiler_params=pltpu.CompilerParams(
+            collective_id=0, has_side_effects=True, vmem_limit_bytes=64 * 2**20
+        ),
+    )(lengths, tokens, cotangent, taps, turned, norm_gains, norm_shifts, by_kind, output_weight, up_weight, down_weight)
+    small = lax.psum(small, "dp")
+    down_grad = lax.psum(down_grad, "dp").astype(F32)
+    up_grad = lax.psum(up_grad, "dp").astype(F32)
+    other_grad = lax.psum(other_grad, "dp").astype(F32)
+    projection_grad = jnp.transpose(other_grad[:, 1:], (0, 2, 1, 3))
+    output_grad = jnp.concatenate([other_grad[:, 0, :columns], other_grad[:, 0, columns:]], axis=2)
+    taps_grad = lax.psum(small[8:, :reach].reshape(LAYERS, heads, reach), "mp")
+    gains_grad = small[0:4].reshape(LAYERS, 2, width)
+    shifts_grad = small[4:8].reshape(LAYERS, 2, width)
+    return (activations, token_grad, projection_grad, taps_grad, output_grad, gains_grad, shifts_grad, up_grad, down_grad)
+
+
 def solution(mesh):
+    fused = mesh.shape["mp"] == 2
+
+    def step(*arrays):
+        return (fused_body if fused else body)(*arrays)
+
     return jax.shard_map(
-        body,
+        step,
         mesh=mesh,
         in_specs=(
             P("dp", None),

time: 1050 us -> 515 us (0.49)
  matrix products: 214 us -> 0 us
  blocking collectives: 169 us -> 8.12 us
  Pallas kernels: 0 us -> 117 us
  waiting for transfers between devices: 439 us -> 340 us
  other arithmetic: 107 us -> 14.1 us
  local copies, waits for them, and re-layouts: 57.2 us -> 11.2 us
  starting transfers between devices: 30.8 us -> 0.08 us
    dot_general x212 -> x0, matrix products: 212 us -> none  [the longest x12 33.2 us: contract(): lax.dot_general(left, right, (((left_dim,), (right_dim,)), ((), ())), pre...]
    pallas_call x0 -> x1, Pallas kernels: none -> 117 us  [fused_body(): pl.pallas_call(whole_step, out_shape=[shape((rows, width), BF16), shape((...]
    all_gather x15 -> x0, blocking collectives: 95 us -> none  [the longest x9 64.3 us: whole_rows(): lax.all_gather(share.astype(jnp.bfloat16), 'mp', axis=0, tiled=True)]
    reduce_scatter x8 -> x0, waiting for transfers between devices: 80.3 us -> none  [row_sums(): lax.psum_scatter(partial_value.astype(jnp.bfloat16), 'mp', scatter_dimens...]
    psum x3 -> x1, blocking collectives: 73.9 us -> 8.12 us  [fused_body(): taps_grad = lax.psum(small[8:, :reach].reshape(LAYERS, heads, reach), 'mp')]
    all_to_all x8 -> x0, waiting for transfers between devices: 41.5 us -> none  [the longest x2 18.9 us: forward_layer(): lax.all_to_all(mixed, 'mp', split_axis=0, concat_axis=2, tiled=True)]
    unnamed x810 -> x16, local copies, waits for them, and re-layouts: 36.5 us -> 3.06 us
    all_to_all x8 -> x0, starting transfers between devices: 29.5 us -> none  [the longest x2 7.83 us: backward_layer(): lax.all_to_all(for_sending(stacked_rows), 'mp', split_axis=2, concat_axis...]
  transfers between devices with their start and end apart: 23 -> 2, of which waited for: 22 -> 2; matrix products, arithmetic and copies ran while one was open for 5% -> 1% of each run, Pallas kernels for 0% -> 0%
where the time goes in v1:
time: 515 us; the launch traced here: 506 us
  waiting for transfers between devices  340 us (66%)
  Pallas kernels  117 us (23%)
  between operations  15.2 us (3%)
  other arithmetic  14.1 us (3%)
  local copies, waits for them, and re-layouts  11.2 us (2%)
  blocking collectives  8.12 us (2%)
    psum x1, waiting for transfers between devices, fused_body(): other_grad = lax.psum(other_grad, 'dp').astype(F32)  251 us
    pallas_call x1, Pallas kernels, fused_body(): pl.pallas_call(whole_step, out_shape=[shape((rows, width), BF16), shape((...  117 us
    psum x1, waiting for transfers between devices, fused_body(): small = lax.psum(small, 'dp')  88.7 us
  transfers between devices with their start and end apart: 2, of which 2 were waited for; matrix products, arithmetic and copies ran while one was open for 1% of the time, Pallas kernels for 0%

profile of v1, /device:TPU:0, one launch (start us, length us, event | category | flops | bytes accessed | tf_op | source)
XLA Modules:
  0.0 505.9 jit_solution(11036648672439525066)
XLA Ops:
  7.2 0.0 all-reduce.6.cloned.1.call-start
  7.9 0.7 copy.23
  8.6 0.1 rev.3
  8.7 0.6 pad.7.taps_ref
  9.3 0.6 pad.8.turned_ref
  9.9 117.3 %shard_map.169 = (bf16[256,768]{1,0:T(8,128)(2,1)}, f32[256,768]{1,0:T(8,128)}, f32[32,768]{1,0:T(8,128)}, bf16[2,1536,768]{2,1,0:T(8,128)(2,1)}, bf16[2,768,153...) custom-call(s32[1]{0:T(128)S(6)} %copy.34.length_ref, bf16[256,768]{1,0:T(8,128)(2,1)} %tokens_ref.1, ...), custom_call_target="tpu_custom_call" | custom-call | tf_op jit(solution)/shard_map/pallas_call | solution.py:1028
  127.2 0.0 all-reduce.6.cloned.1.call-update
  127.2 0.0 all-reduce.8.cloned.1.call-start
  127.3 0.7 all-reduce.8.cloned.1.call-update
  128.0 88.7 %all-reduce.6.cloned.1.call-done = f32[32,768]{1,0:T(8,128)} async-done(((f32[32,768]{1,0:T(8,128)}), f32[32,768]{1,0:T(8,128)}) %all-reduce.6.cloned.1.call-update) | async-done | bytes 98320 | tf_op jit(solution)/shard_map/psum | solution.py:1045
  216.6 0.8 fusion
  217.4 0.6 reshape.29
  218.1 0.7 slice.25
  218.8 8.1 %psum.37 = f32[2,12,33]{2,1,0:T(8,128)S(1)} all-reduce(f32[2,12,33]{2,1,0:T(8,128)S(1)} %reshape.27), channel_id=1, replica_groups=mesh['dp'=16,'mp'=2] {'mp'}, use_global_device_ids=true, to_apply=%region_2.3 | all-reduce | flops 792 | bytes 6336 | tf_op jit(solution)/shard_map/psum | solution.py:1051
  226.9 0.6 copy.26
  227.5 0.6 reshape.28
  228.1 250.6 %all-reduce.8.cloned.1.call-done = (bf16[2,4,768,384]{3,2,1,0:T(8,128)(2,1)}, bf16[2,768,1536]{2,1,0:T(8,128)(2,1)}, bf16[2,1536,768]{2,1,0:T(8,128)(2,1)}) async-done(((bf16[2,4,768,384]{3,2,1,0:T(8,128)(2,1)}, bf16[2,768,1536]{2,1,0:T(8,128)(2,1)}, bf16[2,1536,768]{2,1,0:T(8,128)(2,1)}), (bf16[2,4,768,384]{3,2,1,0:T(8,128)(2,1)}, bf16[2,768,1536]{2,1,0:T(8,128)(2,1)}, ...) | async-done | bytes 14155792 | tf_op jit(solution)/shard_map/psum | solution.py:1048
  478.7 3.0 convert_element_type.12
  481.7 0.0 slice-start.2
  481.7 0.2 slice_bitcast_fusion.2
  481.8 0.0 slice-start.3
  481.8 0.0 slice-start
  481.9 3.9 slice_bitcast_fusion
  485.8 0.0 slice-start.1
  485.8 0.0 slice-done.2
  485.8 0.1 slice-done.3
  485.9 5.1 %convert_element_type.13 = f32[2,768,1536]{2,1,0:T(8,128)} convert(bf16[2,768,1536]{2,1,0:T(8,128)(2,1)S(1)} %bitcast.12) | non-fusion elementwise | flops 2359296 | bytes 14155776 | tf_op jit(solution)/shard_map/convert_element_type | solution.py:1047
  490.9 0.0 slice-done
  490.9 0.0 slice-done.1
  490.9 4.5 convert_element_type.14
  495.4 0.0 copy-start.1
  495.4 0.0 copy-start
  495.4 1.6 pad_maximum_fusion
  497.0 0.0 copy-done.1
  497.0 0.7 copy.35
  497.8 0.0 copy-done
  497.8 0.9 copy.36
  (3 shorter events, 0.0 us)
Async XLA Ops:
  7.2 209.4 %all-reduce.6.cloned.1.call-start = ((), (), s32[]{:S(2)}) async-start(), calls=%async_computation | async-start | bytes 196608 | tf_op jit(solution)/shard_map/psum | solution.py:1045
  127.2 351.5 %all-reduce.8.cloned.1.call-start = ((), (), s32[]{:S(2)}) async-start(), calls=%async_computation.1 | async-start | bytes 28311552 | tf_op jit(solution)/shard_map/psum | solution.py:1048
  481.7 4.1 slice-start.2
  481.8 4.0 slice-start.3
  481.8 9.1 %slice-start = ((s8[4718592]{0:T(1024)(128)(4,1)}), s8[524288]{0:T(1024)(128)(4,1)S(1)}, s32[]{:S(2)}) async-start(s8[4718592]{0:T(1024)(128)(4,1)} %bitcast.9), calls=%async_computation.2 | async-start | bytes 1048576
  485.8 5.2 %slice-start.1 = ((s8[4718592]{0:T(1024)(128)(4,1)}), s8[4194304]{0:T(1024)(128)(4,1)S(1)}, s32[]{:S(2)}) async-start(s8[4718592]{0:T(1024)(128)(4,1)} %bitcast.9), calls=%async_computation.3 | async-start | bytes 8388608
  495.4 1.6 copy-start.1
  495.4 2.3 copy-start
Sparse Core Ops, SparseCore 0:
  127.3 89.2 all-reduce.5
  221.7 256.9 all-reduce.7
